TPU v7x, 32 devices: a whole 2x2x4 slice. The times are simulated.
32 devices in a mesh: dp: 8 (over z, x), ctx: 4 (over y, core).
Axes of the slice: x: 2, y: 2, z: 4, core: 2. Of those that a mesh axis runs over, the one named last changes fastest.
Arguments:
- queries: bfloat16 [8, 896, 1024], P('dp', 'ctx'), may hold values from -5 to 5
- keys: bfloat16 [8, 896, 128], P('dp', 'ctx'), may hold values from -5 to 5
- values: bfloat16 [8, 896, 128], P('dp', 'ctx'), may hold values from -6 to 6
- out_grad: bfloat16 [8, 896, 1024], P('dp', 'ctx'), may hold values from -6 to 6
- segments: int32 [8, 896], P('dp', 'ctx'), may hold values from 0 to 2, never falling along the last dimension, each value on 1 to 672 neighbouring positions
- features: bfloat16 [8, 896, 8192], P('dp', 'ctx'), may hold values from -6 to 6
- projector: bfloat16 [8192, 512], P('dp'), may hold values from -0.25 to 0.25
- first_moment: float32 [512, 256], P(('dp', 'ctx')), may hold values from -10 to 10, as said below
- second_moment: float32 [512, 256], P(('dp', 'ctx')), may hold values from 0.01 to 100
- adam_step: int32 [1], replicated, may hold values from 10 to 1000
Outputs:
- query_grad: bfloat16 [8, 896, 1024], P('dp', 'ctx')
- update: float32 [8192, 256], P(('dp', 'ctx'))
- first_new: float32 [512, 256], P(('dp', 'ctx'))
- second_new: float32 [512, 256], P(('dp', 'ctx'))
Inputs may be any that keep to these rules, and one draw needn't show every extreme that they name: `segments`: segment numbers never fall along a sequence; a document holds 1 to 672 tokens and one holds exactly that many. `first_moment`: each entry's magnitude is at most the square root of the same entry of second_moment.
All inputs are finite; a program needn't handle non-finite values.
Results may differ from a plain program's by a relative error of at most 0.0044.
The roundings to bfloat16 on the way count: a program that leaves them out, or rounds other values in their place, can miss the bound.
Values may be sent and summed in bfloat16 or wider, within the bound.
A program may use at most 64 MiB of HBM per device.

v0:
```python
import math

import jax
import jax.numpy as jnp
from jax import lax
from jax.sharding import PartitionSpec as P

HEADS = 8


BETA_ONE = 0.9
BETA_TWO = 0.999
EPSILON = 1e-08


def shards(
    queries,
    keys,
    values,
    out_grad,
    segments,
    features,
    projector,
    first_moment,
    second_moment,
    adam_step,
):
    tok_rows = queries.shape[1]
    head_size = keys.shape[2]
    scale = 1.0 / math.sqrt(head_size)
    all_keys, all_values, all_segments = (
        lax.all_gather(keys, "ctx", axis=1, tiled=True),
        lax.all_gather(values, "ctx", axis=1, tiled=True),
        lax.all_gather(segments, "ctx", axis=1, tiled=True),
    )
    seq_len = all_keys.shape[1]
    block_len = seq_len if seq_len <= 1024 else 512
    block_count = seq_len // block_len
    query_heads = queries[0].reshape(tok_rows, HEADS, head_size)
    grad_heads = out_grad[0].reshape(tok_rows, HEADS, head_size)
    own_segments = segments[0]
    query_pos = lax.axis_index("ctx") * tok_rows + jnp.arange(tok_rows, dtype=jnp.int32)
    last_pos = query_pos[tok_rows - 1]
    key_blocks = all_keys[0].reshape(block_count, block_len, head_size)
    value_blocks = all_values[0].reshape(block_count, block_len, head_size)
    segment_blocks = all_segments[0].reshape(block_count, block_len)
    block_starts = jnp.arange(block_count, dtype=jnp.int32) * block_len

    def block_terms(key_block, value_block, segment_block, block_start):
        key_pos = block_start + jnp.arange(block_len, dtype=jnp.int32)
        allowed = (key_pos[None, :] <= query_pos[:, None]) & (
            segment_block[None, :] == own_segments[:, None]
        )
        scores = (
            jnp.einsum("thd,kd->thk", query_heads, key_block, preferred_element_type=jnp.float32)
            * scale
        )
        masked = jnp.where(allowed[:, None, :], scores, -jnp.inf)
        dprob = jnp.einsum(
            "thd,kd->thk", grad_heads, value_block, preferred_element_type=jnp.float32
        )
        return (masked, dprob)

    def first_pass(carry, block_in):
        key_block, value_block, segment_block, block_start = block_in

        def first_live_block(state):
            row_top, total, weighted = state
            masked, dprob = block_terms(key_block, value_block, segment_block, block_start)
            new_top = jnp.maximum(row_top, jnp.max(masked, axis=2))
            factor = jnp.exp(row_top - new_top)
            expo = jnp.exp(masked - new_top[:, :, None])
            total = total * factor + jnp.sum(expo, axis=2)
            weighted = weighted * factor + jnp.sum(expo * dprob, axis=2)
            return (new_top, total, weighted)

        def first_masked_block(state):
            return state

        return (lax.cond(block_start > last_pos, first_masked_block, first_live_block, carry), None)

    start_carry = (
        jnp.full((tok_rows, HEADS), -1e30, jnp.float32),
        jnp.zeros((tok_rows, HEADS), jnp.float32),
        jnp.zeros((tok_rows, HEADS), jnp.float32),
    )
    (row_top, total, weighted), unused = lax.scan(
        first_pass, start_carry, (key_blocks, value_blocks, segment_blocks, block_starts)
    )
    log_total = row_top + jnp.log(total)
    delta = weighted / total

    def second_pass(query_acc, block_in):
        key_block, value_block, segment_block, block_start = block_in

        def second_live_block(acc_now):
            masked, dprob = block_terms(key_block, value_block, segment_block, block_start)
            probs = jnp.exp(masked - log_total[:, :, None])
            dscore = (probs * (dprob - delta[:, :, None])).astype(jnp.bfloat16)
            probs_low = probs.astype(jnp.bfloat16)
            acc_now = acc_now + jnp.einsum(
                "thk,kd->thd", dscore, key_block, preferred_element_type=jnp.float32
            )
            key_part = (
                jnp.einsum("thk,thd->kd", dscore, query_heads, preferred_element_type=jnp.float32)
                * scale
            )
            value_part = jnp.einsum(
                "thk,thd->kd", probs_low, grad_heads, preferred_element_type=jnp.float32
            )
            return (acc_now, jnp.concatenate([key_part, value_part], axis=1))

        def second_masked_block(acc_now):
            return (acc_now, jnp.zeros((block_len, 2 * head_size), jnp.float32))

        return lax.cond(block_start > last_pos, second_masked_block, second_live_block, query_acc)

    query_acc, kv_terms = lax.scan(
        second_pass,
        jnp.zeros((tok_rows, HEADS, head_size), jnp.float32),
        (key_blocks, value_blocks, segment_blocks, block_starts),
    )
    query_grad = (query_acc * scale).reshape(1, tok_rows, HEADS * head_size).astype(jnp.bfloat16)
    kv_partial = kv_terms.reshape(seq_len, 2 * head_size)
    kv_grad = lax.psum_scatter(kv_partial, "ctx", scatter_dimension=0, tiled=True).astype(
        jnp.bfloat16
    )
    feature_rows = features[0]
    width = feature_rows.shape[1]
    device_count = lax.axis_size("dp") * lax.axis_size("ctx")
    slab_rows = width // device_count
    projector_slab = lax.dynamic_slice_in_dim(
        projector, lax.axis_index("ctx") * slab_rows, slab_rows, 0
    )
    projector_wide = projector_slab.astype(jnp.float32)
    grad_slab = lax.psum_scatter(
        jnp.einsum("td,tc->dc", feature_rows, kv_grad, preferred_element_type=jnp.float32),
        ("dp", "ctx"),
        scatter_dimension=0,
        tiled=True,
    )
    partial_proj = jnp.dot(projector_wide.T, grad_slab, precision=lax.Precision.HIGHEST)
    projected = lax.psum_scatter(partial_proj, ("dp", "ctx"), scatter_dimension=0, tiled=True)
    first_new = BETA_ONE * first_moment + (1.0 - BETA_ONE) * projected
    second_new = BETA_TWO * second_moment + (1.0 - BETA_TWO) * projected * projected
    step_count = adam_step[0].astype(jnp.float32)
    bias_first = 1.0 - jnp.power(jnp.float32(BETA_ONE), step_count)
    bias_second = 1.0 - jnp.power(jnp.float32(BETA_TWO), step_count)
    direction = first_new / bias_first / (jnp.sqrt(second_new / bias_second) + EPSILON)
    whole_direction = lax.all_gather(direction, ("dp", "ctx"), axis=0, tiled=True)
    update = jnp.dot(projector_wide, whole_direction, precision=lax.Precision.HIGHEST)
    return (query_grad, update, first_new, second_new)


def solution(mesh):
    in_specs = (
        P("dp", "ctx", None),
        P("dp", "ctx", None),
        P("dp", "ctx", None),
        P("dp", "ctx", None),
        P("dp", "ctx"),
        P("dp", "ctx", None),
        P("dp", None),
        P(("dp", "ctx"), None),
        P(("dp", "ctx"), None),
        P(),
    )
    out_specs = (
        P("dp", "ctx", None),
        P(("dp", "ctx"), None),
        P(("dp", "ctx"), None),
        P(("dp", "ctx"), None),
    )
    return jax.shard_map(shards, mesh=mesh, in_specs=in_specs, out_specs=out_specs, check_vma=False)
```

profile of v0, /device:TPU:1, one launch (start us, length us, event | category | flops | bytes accessed | tf_op | source)
XLA Modules:
  0.0 413.6 jit_solution(7261736164223633094)
XLA Ops:
  8.5 1.2 dynamic-slice
  11.3 5.1 %all-reduce = s32[896]{0:T(1024)S(1)} all-reduce(s32[896]{0:T(1024)S(1)} %dynamic-update-slice), channel_id=1, replica_groups=mesh['dp'=8,'ctx'=4] {'ctx'}, use_global_device_ids=true, to_apply=%add | all-reduce | flops 896 | bytes 7168 | tf_op jit(solution)/shard_map/while/body/jit(dynamic_index_in_dim)/squeeze | solution.py:87
  16.4 7.1 %all_gather.13 = bf16[1,896,128]{2,1,0:T(8,128)(2,1)S(1)} all-gather(bf16[1,224,128]{2,1,0:T(8,128)(2,1)} %param.15), channel_id=1, replica_groups=mesh['dp'=8,'ctx'=4] {'ctx'}, dimensions={1}, use_global_device_ids=true | all-gather | bytes 286720 | tf_op jit(solution)/shard_map/all_gather | solution.py:32
  23.4 5.9 %all_gather.14 = bf16[1,896,128]{2,1,0:T(8,128)(2,1)S(1)} all-gather(bf16[1,224,128]{2,1,0:T(8,128)(2,1)} %param.16), channel_id=1, replica_groups=mesh['dp'=8,'ctx'=4] {'ctx'}, dimensions={1}, use_global_device_ids=true | all-gather | bytes 286720 | tf_op jit(solution)/shard_map/all_gather | solution.py:33
  29.3 1.1 copy.28
  30.4 1.9 copy.29
  32.3 8.6 %conditional.2 = (f32[224,8]{1,0:T(8,128)S(1)}, f32[224,8]{1,0:T(8,128)S(1)}, f32[224,8]{1,0:T(8,128)S(1)}) conditional(s32[]{:T(128)} %bitcast.8, (s32[224]{0:T(256)S(1)}, s32[896]{0:T(1024)S(1)}, s32[1,224]{1,0:T(1,128)}, bf16[224,8,128]{2,1,0:T(8,128)(2,1)S(1)}, bf16[896,128]{1,0:T(8,128)(2,1)S(1)}, /*index=5*/f32[224,8]{1,0:T(8,128)S(1)}, ...), branch_computations={%region_0.4_spmd, %region_4.5_spmd} | conditional | flops 841956864 | bytes 21559576 | solution.py:80
  33.3 1.8 fusion
  35.1 3.5 multiply_reduce_fusion
  38.6 2.2 fusion.1
  41.0 11.0 %conditional.3 = (f32[224,8,128]{2,1,0:T(8,128)S(1)}, f32[896,256]{0,1:T(8,128)S(1)}) conditional(s32[]{:T(128)} %bitcast.8, (s32[224]{0:T(256)S(1)}, s32[896]{0:T(1024)S(1)}, s32[1,224]{1,0:T(1,128)}, bf16[224,8,128]{2,1,0:T(8,128)(2,1)S(1)}, bf16[896,128]{1,0:T(8,128)(2,1)S(1)}, /*index=5*/f32[224,8]{1,0:T(8,128)S(1)}, f32[224,8]{1,0:T(8,128)S(1)}, ...), branch_computations={%region_5.6_spmd, %region_6.7_spmd} | conditional | flops 2072444416 | bytes 36676880 | solution.py:116
  43.2 3.1 fusion.13
  46.3 3.6 multiply_convert_fusion
  49.9 1.3 convolution_add_fusion
  52.0 1.2 copy.26
  53.3 24.3 %reduce-scatter.10.cloned.1.call-done = f32[224,256]{1,0:T(8,128)} async-done(((f32[896,256]{1,0:T(8,128)}), f32[224,256]{1,0:T(8,128)}) %reduce-scatter.10.cloned.1.call-update) | async-done | bytes 229392
  77.6 1.0 copy.27
  78.6 6.5 %convolution_bitcast_fusion.1 = f32[8192,256]{0,1:T(8,128)} fusion(bf16[1,224,8192]{2,1,0:T(8,128)(2,1)} %param.19, bf16[224,256]{0,1:T(8,128)(2,1)S(1)} %copy.27), kind=kOutput, calls=%fused_computation.32 | convolution fusion | flops 939524096 | bytes 12173312 | tf_op jit(solution)/shard_map/td,tc->dc/dot_general | solution.py:137
  85.2 143.4 %reduce-scatter.6.cloned.1.call-done = f32[256,256]{0,1:T(8,128)} async-done(((f32[8192,256]{0,1:T(8,128)}), f32[256,256]{0,1:T(8,128)}) %reduce-scatter.6.cloned.1.call-update) | async-done | bytes 262160 | tf_op jit(solution)/shard_map/reduce_scatter | solution.py:136
  228.6 2.2 fusion.26
  232.6 128.5 %reduce-scatter.8.cloned.1.call-done = f32[16,256]{1,0:T(8,128)} async-done(((f32[512,256]{1,0:T(8,128)}), f32[16,256]{1,0:T(8,128)}) %reduce-scatter.8.cloned.1.call-update) | async-done | bytes 16400 | tf_op jit(solution)/shard_map/reduce_scatter | solution.py:143
  361.2 1.3 multiply_divide_fusion
  362.5 43.5 %all_gather.15 = f32[512,256]{1,0:T(8,128)S(1)} all-gather(f32[16,256]{1,0:T(8,128)S(1)} %get-tuple-element.184), channel_id=1, replica_groups=mesh['dp'=8,'ctx'=4] {'dp','ctx'}, dimensions={0}, use_global_device_ids=true | all-gather | bytes 540672 | tf_op jit(solution)/shard_map/all_gather | solution.py:150
  406.0 1.1 fusion.24
  (29 shorter events, 6.5 us)
Async XLA Ops:
  7.2 221.5 %copy-start = (bf16[1024,512]{1,0:T(8,128)(2,1)S(1)}, bf16[1024,512]{1,0:T(8,128)(2,1)}, u32[]{:S(2)}) copy-start(bf16[1024,512]{1,0:T(8,128)(2,1)} %param.20) | copy-start | bytes 3145732
  7.2 70.4 %reduce-scatter.10.cloned.1.call-start = ((), (), s32[]{:S(2)}) async-start(), calls=%async_computation.5 | async-start | bytes 1146880
  53.2 175.4 %reduce-scatter.6.cloned.1.call-start = ((), (), s32[]{:S(2)}) async-start(), calls=%async_computation.3 | async-start | bytes 8650752 | tf_op jit(solution)/shard_map/reduce_scatter | solution.py:136
  85.1 276.0 %copy-start.1 = (f32[16,256]{1,0:T(8,128)S(1)}, f32[16,256]{1,0:T(8,128)}, u32[]{:S(2)}) copy-start(f32[16,256]{1,0:T(8,128)} %param.22) | copy-start | bytes 49156
  85.1 276.0 %copy-start.2 = (f32[16,256]{1,0:T(8,128)S(1)}, f32[16,256]{1,0:T(8,128)}, u32[]{:S(2)}) copy-start(f32[16,256]{1,0:T(8,128)} %param.21) | copy-start | bytes 49156
  85.2 276.0 %reduce-scatter.8.cloned.1.call-start = ((), (), s32[]{:S(2)}) async-start(), calls=%async_computation.4 | async-start | bytes 540672 | tf_op jit(solution)/shard_map/reduce_scatter | solution.py:143
Sparse Core Ops, SparseCore 0:
  53.4 24.1 reduce-scatter.9
  85.3 143.2 reduce-scatter.5
  231.0 130.1 reduce-scatter.7
where the time goes:
time: 414 us
  waiting for transfers between devices  296 us (71%)
  blocking collectives  61.5 us (15%)
  matrix products  24.9 us (6%)
  between operations  15.9 us (4%)
  local copies, waits for them, and re-layouts  9 us (2%)
  other arithmetic  5.68 us (1%)
    reduce_scatter x1, waiting for transfers between devices, shards(): lax.psum_scatter(jnp.einsum('td,tc->dc', feature_rows, kv_grad, preferred...  143 us
    reduce_scatter x1, waiting for transfers between devices, shards(): lax.psum_scatter(partial_proj, ('dp', 'ctx'), scatter_dimension=0, tiled=...  129 us
    all_gather x1, blocking collectives, shards(): lax.all_gather(direction, ('dp', 'ctx'), axis=0, tiled=True)  43.5 us
    unnamed x4, waiting for transfers between devices  24.3 us
  transfers between devices with their start and end apart: 3, of which 3 were waited for; matrix products, arithmetic and copies ran while one was open for 0% of the time, Pallas kernels for 0%

commit v1 on v0

v1 whole, which is shorter than its diff:
```python
import functools
import math

import jax
import jax.numpy as jnp
from jax import lax
from jax.experimental import pallas as pl
from jax.experimental.pallas import tpu as pltpu
from jax.sharding import PartitionSpec as P

HEADS = 8
BETA_ONE = 0.9
BETA_TWO = 0.999
EPSILON = 1e-08
MESH = pl.DeviceIdType.MESH
F32 = jnp.float32
BF16 = jnp.bfloat16


def dot_nt(a, b):
    return lax.dot_general(a, b, (((1,), (1,)), ((), ())), preferred_element_type=F32)


def dot_tn(a, b):
    return lax.dot_general(a, b, (((0,), (0,)), ((), ())), preferred_element_type=F32)


def dot_nn(a, b):
    return jnp.dot(a, b, preferred_element_type=F32)


def split_two(x):
    high = x.astype(BF16)
    return high, (x - high.astype(F32)).astype(BF16)


def body(
    n_dp,
    n_ctx,
    group,
    q_ref,
    k_ref,
    v_ref,
    og_ref,
    seg_row_ref,
    seg_col_ref,
    f_ref,
    p_ref,
    m1_ref,
    m2_ref,
    bias_ref,
    qg_ref,
    up_ref,
    m1_out,
    m2_out,
    qs,
    gs,
    kall,
    vall,
    seg_all,
    kvacc,
    kv_in,
    kv_pair,
    pall,
    fcat,
    gacc,
    pp,
    cx,
    sb,
    rb,
    dall,
    dother,
    dfull,
    kvs_send,
    kvs_recv,
    rs_send,
    rs_recv,
    p_send,
    p_recv,
    one_send,
    one_recv,
    local_sem,
    red_send,
    red_recv,
    dir_send,
    dir_recv,
):
    tok = q_ref.shape[0]
    hd = k_ref.shape[1]
    seq = n_ctx * tok
    scale = 1.0 / math.sqrt(hd)
    d = lax.axis_index("dp")
    c = lax.axis_index("ctx")
    core = lax.rem(c, 2)
    other = c + 1 - 2 * core
    half_ctx = n_ctx // 2
    chips = n_dp * half_ctx
    chip = d * half_ctx + c // 2
    side = lax.rem(d, 2)
    line = d // 2
    lines = n_dp // 2
    mate = d + 1 - 2 * side
    slab = p_ref.shape[0]
    half = slab // 2
    rows = m1_ref.shape[0]

    barrier = pltpu.get_barrier_semaphore()

    def chip_device(index):
        return (index // half_ctx, lax.rem(index, half_ctx) * 2 + core)

    @pl.loop(1, chips)
    def _(step):
        pl.semaphore_signal(
            barrier, inc=1, device_id=chip_device(lax.rem(chip + step, chips)), device_id_type=MESH
        )

    @pl.loop(0, half_ctx)
    def _(step):
        pl.semaphore_signal(
            barrier, inc=1, device_id=(d, step * 2 + 1 - core), device_id_type=MESH
        )

    def remote(src, dst, send, recv, device):
        return pltpu.make_async_remote_copy(
            src_ref=src, dst_ref=dst, send_sem=send, recv_sem=recv, device_id=device, device_id_type=MESH
        )

    def own_feature_copy(index):
        return pltpu.make_async_copy(
            f_ref.at[:, pl.ds(pl.multiple_of(index * slab + core * half, half), half)],
            fcat.at[0, :, pl.ds(index * half, half)],
            local_sem,
        )

    for index in range(n_dp):
        own_feature_copy(index).start()
    pall[d] = p_ref[pl.ds(pl.multiple_of(core * half, half), half), :]
    kall[c] = k_ref[...]
    vall[c] = v_ref[...]
    seg_all[c] = seg_row_ref[...]
    for head in range(HEADS):
        qs[head * tok : (head + 1) * tok, :] = q_ref[:, head * hd : (head + 1) * hd]
        gs[head * tok : (head + 1) * tok, :] = og_ref[:, head * hd : (head + 1) * hd]
    pl.semaphore_wait(barrier, chips - 1 + half_ctx)

    def kvs_copies(step):
        to = lax.rem(c + step, n_ctx)
        return [
            remote(buf.at[c], buf.at[c], kvs_send.at[i, step], kvs_recv.at[i, c], (d, to))
            for i, buf in enumerate((seg_all, kall, vall))
        ]

    for step in range(1, n_ctx):
        for copy in kvs_copies(step):
            copy.start()

    def p_copy(index, way, device_dp):
        return remote(
            pall.at[index], pall.at[index], p_send.at[way, index], p_recv.at[index], (device_dp, c)
        )

    p_copy(d, 2, mate).start()

    @pl.when(line + 1 < lines)
    def _():
        p_copy(d, 0, d + 2).start()

    @pl.when(line > 0)
    def _():
        p_copy(d, 1, d - 2).start()

    def feature_copy(index):
        return remote(
            f_ref.at[:, pl.ds(pl.multiple_of(index * slab + (1 - core) * half, half), half)],
            fcat.at[1, :, pl.ds(index * half, half)],
            one_send.at[0],
            one_recv.at[0],
            (d, other),
        )

    for index in range(n_dp):
        feature_copy(index).start()

    def p_arrived(index):
        p_copy(index, 2, mate).wait_recv()

    def project(index):
        piece = pall[index]
        cols = pl.ds(pl.multiple_of(index * half, half), half)
        gacc[0] += dot_nn(fcat[0, :, cols], piece)
        gacc[1] += dot_nn(fcat[1, :, cols], piece)

    def forward(distance):
        src = line - distance

        @pl.when(src >= 0)
        def _():
            index = src * 2 + side
            p_arrived(index)

            @pl.when(line + 1 < lines)
            def _():
                p_copy(index, 0, d + 2).start()

            p_copy(index, 2, mate).start()

        back = line + distance

        @pl.when(back < lines)
        def _():
            index = back * 2 + side
            p_arrived(index)

            @pl.when(line > 0)
            def _():
                p_copy(index, 1, d - 2).start()

            p_copy(index, 2, mate).start()

    def project_line(distance):
        @pl.when(line - distance >= 0)
        def _():
            project((line - distance) * 2 + side)

        @pl.when(line + distance < lines)
        def _():
            project((line + distance) * 2 + side)

    def project_across(distance):
        @pl.when(line - distance >= 0)
        def _():
            index = (line - distance) * 2 + 1 - side
            p_arrived(index)
            project(index)

        if distance > 0:

            @pl.when(line + distance < lines)
            def _():
                index = (line + distance) * 2 + 1 - side
                p_arrived(index)
                project(index)

    for step in range(1, n_ctx):
        source = lax.rem(c + n_ctx - step, n_ctx)
        for i, buf in enumerate((seg_all, kall, vall)):
            remote(
                buf.at[source], buf.at[source], kvs_send.at[i, step], kvs_recv.at[i, source], (d, other)
            ).wait_recv()

    width = group * tok
    starts = jnp.zeros((8, width), F32)
    ones = jnp.ones((8, tok), BF16)
    for block in range(n_ctx):
        below = jnp.where(seg_all[block] < seg_col_ref[...], 1.0, 0.0).astype(BF16)
        starts = starts + dot_nt(ones, below)
    first_key = starts[0:1, :].astype(jnp.int32)
    lane = lax.broadcasted_iota(jnp.int32, (1, width), 1)
    query_pos = c * tok + lax.rem(lane, tok)
    key_pos = lax.broadcasted_iota(jnp.int32, (seq, width), 0)

    def attend(index):
        at = index * group * tok
        keys = kall[...].reshape(seq, hd)
        vals = vall[...].reshape(seq, hd)
        q_now = qs[at : at + width, :]
        g_now = gs[at : at + width, :]
        allowed = (key_pos <= query_pos) & (key_pos >= first_key)
        scores = jnp.where(allowed, dot_nt(keys, q_now) * scale, -1e30)
        top = jnp.max(scores, axis=0, keepdims=True)
        expo = jnp.exp(scores - top)
        inverse = 1.0 / jnp.sum(expo, axis=0, keepdims=True)
        dprob = dot_nt(vals, g_now)
        probs = expo * inverse
        delta = jnp.sum(probs * dprob, axis=0, keepdims=True)
        dscore = (probs * (dprob - delta)).astype(BF16)
        probs_low = probs.astype(BF16)
        dk = (dot_nn(dscore, q_now) * scale).reshape(n_ctx, tok, hd)
        dv = dot_nn(probs_low, g_now).reshape(n_ctx, tok, hd)
        if index == 0:
            kvacc[:, :, 0:hd] = dk
            kvacc[:, :, hd : 2 * hd] = dv
        else:
            kvacc[:, :, 0:hd] += dk
            kvacc[:, :, hd : 2 * hd] += dv
        dq = (dot_tn(dscore, keys) * scale).astype(BF16)
        for h in range(group):
            head = index * group + h
            qg_ref[:, head * hd : (head + 1) * hd] = dq[h * tok : (h + 1) * tok, :]

    groups = HEADS // group
    for index in range(groups):
        attend(index)
        if index == 0 and lines > 1:
            forward(1)

    def kv_copy(step):
        to = lax.rem(c + step, n_ctx)
        return remote(kvacc.at[to], kv_in.at[c], rs_send.at[step], rs_recv.at[c], (d, to))

    for step in range(1, n_ctx):
        kv_copy(step).start()

    pltpu.make_async_copy(fcat.at[0], fcat.at[0], local_sem).wait()
    remote(fcat.at[1], fcat.at[1], one_send.at[0], one_recv.at[0], (d, other)).wait_recv()
    gacc[...] = jnp.zeros_like(gacc)
    project(d)
    project_across(0)
    if lines > 1:
        project_line(1)
    if lines > 2:
        forward(2)

    total = kvacc[c]
    for step in range(1, n_ctx):
        source = lax.rem(c + n_ctx - step, n_ctx)
        remote(
            kv_in.at[source], kv_in.at[source], rs_send.at[step], rs_recv.at[source], (d, other)
        ).wait_recv()
        total = total + kv_in[source]
    kv_pair[0] = total.astype(BF16)
    kv_copy_pair = remote(
        kv_pair.at[0], kv_pair.at[1], one_send.at[1], one_recv.at[1], (d, other)
    )
    kv_copy_pair.start()

    for distance in range(1, lines):
        if distance > 2:
            forward(distance)
        if distance > 1:
            project_line(distance)
        project_across(distance)
    kv_copy_pair.wait()

    term = jnp.zeros((gacc.shape[2], 2 * hd), F32)
    for part in range(2):
        high, low = split_two(gacc[part])
        kv_now = kv_pair[part]
        term = term + dot_tn(high, kv_now) + dot_tn(low, kv_now)
    for index in range(chips):
        for k in range(2):
            at = (index * 2 + k) * rows
            pp[k, index] = term[at : at + rows, :]
    swap = remote(pp.at[1 - core], cx, one_send.at[2], one_recv.at[2], (d, other))
    swap.start()
    swap.wait()
    sb[...] = pp[core] + cx[...]

    def sum_copy(step):
        to = lax.rem(chip + step, chips)
        return remote(
            sb.at[to], rb.at[chip], red_send.at[step], red_recv.at[chip], chip_device(to)
        )

    @pl.loop(1, chips)
    def _(step):
        sum_copy(step).start()

    rb[chip] = sb[chip]

    @pl.loop(1, chips)
    def _(step):
        source = lax.rem(chip + chips - step, chips)
        remote(
            rb.at[source], rb.at[source], red_send.at[step], red_recv.at[source], chip_device(source)
        ).wait_recv()

    projected = jnp.sum(rb[...], axis=0)
    first_new = BETA_ONE * m1_ref[...] + (1.0 - BETA_ONE) * projected
    second_new = BETA_TWO * m2_ref[...] + (1.0 - BETA_TWO) * projected * projected
    bias_first = bias_ref[0:1, 0:1]
    bias_second = bias_ref[0:1, 1:2]
    m1_out[...] = first_new
    m2_out[...] = second_new
    dall[chip] = first_new / bias_first / (jnp.sqrt(second_new / bias_second) + EPSILON)

    def dir_copy(step):
        to = lax.rem(chip + step, chips)
        return remote(
            dall.at[chip], dall.at[chip], dir_send.at[step], dir_recv.at[chip], chip_device(to)
        )

    @pl.loop(1, chips)
    def _(step):
        dir_copy(step).start()

    @pl.loop(1, chips)
    def _(step):
        source = lax.rem(chip + chips - step, chips)
        remote(
            dall.at[source], dall.at[source], dir_send.at[step], dir_recv.at[source], chip_device(source)
        ).wait_recv()

    swap_dir = remote(dall, dother, one_send.at[3], one_recv.at[3], (d, other))
    swap_dir.start()
    swap_dir.wait()
    even = jnp.where(core == 0, dall[...], dother[...])
    odd = jnp.where(core == 0, dother[...], dall[...])
    for index in range(chips):
        at = index * 2 * rows
        dfull[at : at + rows, :] = even[index]
        dfull[at + rows : at + 2 * rows, :] = odd[index]
    high, low = split_two(dfull[...])
    out_rows = up_ref.shape[0]
    p_rows = p_ref[pl.ds(pl.multiple_of(c * out_rows, out_rows), out_rows), :]
    up_ref[...] = dot_nn(p_rows, high) + dot_nn(p_rows, low)

    for step in range(1, n_ctx):
        for copy in kvs_copies(step):
            copy.wait_send()
        kv_copy(step).wait_send()
    remote(fcat.at[1], fcat.at[1], one_send.at[0], one_recv.at[0], (d, other)).wait_send()

    @pl.loop(1, chips)
    def _(step):
        sum_copy(step).wait_send()
        dir_copy(step).wait_send()

    for distance in range(lines):
        src = line - distance
        back = line + distance

        @pl.when(src >= 0)
        def _():
            p_copy(src * 2 + side, 2, mate).wait_send()

            @pl.when(line + 1 < lines)
            def _():
                p_copy(src * 2 + side, 0, d + 2).wait_send()

        @pl.when(back < lines)
        def _():
            if distance > 0:
                p_copy(back * 2 + side, 2, mate).wait_send()

            @pl.when(line > 0)
            def _():
                p_copy(back * 2 + side, 1, d - 2).wait_send()


def shards(
    n_dp,
    n_ctx,
    queries,
    keys,
    values,
    out_grad,
    segments,
    features,
    projector,
    first_moment,
    second_moment,
    adam_step,
):
    tok, hd = keys.shape[1], keys.shape[2]
    width = features.shape[2]
    slab, rank = projector.shape
    rows, kvw = first_moment.shape
    chips = n_dp * n_ctx // 2
    half = slab // 2
    group = 4 if n_ctx * tok <= 1024 else 1
    step_count = adam_step[0].astype(F32)
    bias = jnp.stack(
        [
            1.0 - jnp.power(F32(BETA_ONE), step_count),
            1.0 - jnp.power(F32(BETA_TWO), step_count),
        ]
    ).reshape(1, 2)
    seg_col = jnp.tile(segments.reshape(tok, 1), (group, 1))
    vmem = pl.BlockSpec(memory_space=pltpu.VMEM)
    hbm = pl.BlockSpec(memory_space=pl.ANY)
    dma = pltpu.SemaphoreType.DMA
    query_grad, update, first_new, second_new = pl.pallas_call(
        functools.partial(body, n_dp, n_ctx, group),
        out_shape=(
            jax.ShapeDtypeStruct((tok, HEADS * hd), BF16),
            jax.ShapeDtypeStruct((width // (n_dp * n_ctx), kvw), F32),
            jax.ShapeDtypeStruct((rows, kvw), F32),
            jax.ShapeDtypeStruct((rows, kvw), F32),
        ),
        in_specs=[vmem] * 6 + [hbm] + [vmem] * 4,
        out_specs=[vmem] * 4,
        scratch_shapes=[
            pltpu.VMEM((HEADS * tok, hd), BF16),
            pltpu.VMEM((HEADS * tok, hd), BF16),
            pltpu.VMEM((n_ctx, tok, hd), BF16),
            pltpu.VMEM((n_ctx, tok, hd), BF16),
            pltpu.VMEM((n_ctx, 1, tok), jnp.int32),
            pltpu.VMEM((n_ctx, tok, kvw), F32),
            pltpu.VMEM((n_ctx, tok, kvw), F32),
            pltpu.VMEM((2, tok, kvw), BF16),
            pltpu.VMEM((n_dp, half, rank), BF16),
            pltpu.VMEM((2, tok, width // 2), BF16),
            pltpu.VMEM((2, tok, rank), F32),
            pltpu.VMEM((2, chips, rows, kvw), F32),
            pltpu.VMEM((chips, rows, kvw), F32),
            pltpu.VMEM((chips, rows, kvw), F32),
            pltpu.VMEM((chips, rows, kvw), F32),
            pltpu.VMEM((chips, rows, kvw), F32),
            pltpu.VMEM((chips, rows, kvw), F32),
            pltpu.VMEM((rank, kvw), F32),
            dma((3, n_ctx)),
            dma((3, n_ctx)),
            dma((n_ctx,)),
            dma((n_ctx,)),
            dma((3, n_dp)),
            dma((n_dp,)),
            dma((4,)),
            dma((4,)),
            dma(()),
            dma((chips,)),
            dma((chips,)),
            dma((chips,)),
            dma((chips,)),
        ],
        compiler_params=pltpu.CompilerParams(
            collective_id=0, has_side_effects=True, vmem_limit_bytes=56 * 2**20
        ),
    )(
        queries[0],
        keys[0],
        values[0],
        out_grad[0],
        segments,
        seg_col,
        features[0],
        projector,
        first_moment,
        second_moment,
        bias,
    )
    return (query_grad[None], update, first_new, second_new)


def solution(mesh):
    in_specs = (
        P("dp", "ctx", None),
        P("dp", "ctx", None),
        P("dp", "ctx", None),
        P("dp", "ctx", None),
        P("dp", "ctx"),
        P("dp", "ctx", None),
        P("dp", None),
        P(("dp", "ctx"), None),
        P(("dp", "ctx"), None),
        P(),
    )
    out_specs = (
        P("dp", "ctx", None),
        P(("dp", "ctx"), None),
        P(("dp", "ctx"), None),
        P(("dp", "ctx"), None),
    )
    fn = functools.partial(shards, mesh.shape["dp"], mesh.shape["ctx"])
    return jax.shard_map(fn, mesh=mesh, in_specs=in_specs, out_specs=out_specs, check_vma=False)
```

time: 414 us -> 86.1 us (0.21)
  waiting for transfers between devices: 296 us -> 0 us
  Pallas kernels: 0 us -> 75.8 us
  blocking collectives: 61.5 us -> 0 us
  matrix products: 24.9 us -> 0 us
  between operations: 15.9 us -> 1.37 us
  other arithmetic: 5.68 us -> 0.59 us
    reduce_scatter x2 -> x0, waiting for transfers between devices: 272 us -> none  [the longest x1 143 us: shards(): lax.psum_scatter(jnp.einsum('td,tc->dc', feature_rows, kv_grad, preferred...]
    pallas_call x0 -> x1, Pallas kernels: none -> 75.8 us  [shards(): pl.pallas_call(functools.partial(body, n_dp, n_ctx, group), out_shape=(ja...]
    all_gather x3 -> x0, blocking collectives: 56.4 us -> none  [the longest x1 43.5 us: shards(): lax.all_gather(direction, ('dp', 'ctx'), axis=0, tiled=True)]
    dot_general x10 -> x0, matrix products: 24.9 us -> none  [the longest x2 7.12 us: block_terms(): jnp.einsum('thd,kd->thk', grad_heads, value_block, preferred_element_type...]
    unnamed x4 -> x0, waiting for transfers between devices: 24.3 us -> none
    squeeze x1 -> x0, blocking collectives: 5.09 us -> none  [shards(): lax.scan(first_pass, start_carry, (key_blocks, value_blocks, segment_bloc...]
  transfers between devices with their start and end apart: 3 -> 0, of which waited for: 3 -> 0; matrix products, arithmetic and copies ran while one was open for 0% -> 0% of each run, Pallas kernels for 0% -> 0%
where the time goes in v1:
time: 86.1 us; the launch traced here: 85.6 us
  Pallas kernels  75.8 us (88%)
  local copies, waits for them, and re-layouts  7.89 us (9%)
  between operations  1.37 us (2%)
    pallas_call x1, Pallas kernels, shards(): pl.pallas_call(functools.partial(body, n_dp, n_ctx, group), out_shape=(ja...  75.8 us
    unnamed x4, local copies, waits for them, and re-layouts  6.13 us
    another operation x2, local copies, waits for them, and re-layouts, shards(): seg_col = jnp.tile(segments.reshape(tok, 1), (group, 1))  1.76 us

profile of v1, /device:TPU:1, one launch (start us, length us, event | category | flops | bytes accessed | tf_op | source)
XLA Modules:
  0.0 85.6 jit_solution(4956083778102021511)
XLA Ops:
  1.4 0.6 maximum_bitcast_fusion.bias_ref
  1.9 0.7 tile.11
  2.6 1.1 %tile.13.seg_col_ref = s32[896,1]{1,0:T(8,128)} reshape(s32[4,224]{1,0:T(4,128)S(1)} %tile.11) | data formatting | bytes 7168 | tf_op jit(solution)/shard_map/tile | solution.py:470
  3.7 75.8 %shard_map.129 = (bf16[224,1024]{1,0:T(8,128)(2,1)}, f32[256,256]{1,0:T(8,128)}, f32[16,256]{1,0:T(8,128)}, f32[16,256]{1,0:T(8,128)}) custom-call(bf16[224,1024]{1,0:T(8,128)(2,1)} %bitcast.11, bf16[224,128]{1,0:T(8,128)(2,1)} %bitcast.13, bf16[224,128]{1,0:T(8,128)(2,1)} %bitcast.14, bf16[224,1024]{1,0:T(8,128)(2,1)} %bitcast.12, s32[1,224]{1,0:T(1,128)} %seg_row_ref.1, ...), custom_call_target="tpu_custom_call" | custom-call | tf_op jit(solution)/shard_map/pallas_call | solution.py:474
  79.5 1.8 %copy.20 = bf16[1,224,1024]{2,1,0:T(8,128)(2,1)} copy(bf16[1,224,1024]{2,1,0:T(8,128)(2,1)} %bitcast.10) | data formatting | bytes 917504
  81.3 1.7 %copy.21 = f32[256,256]{1,0:T(8,128)} copy(f32[256,256]{1,0:T(8,128)} %get-tuple-element.17) | data formatting | bytes 524288
  83.0 1.3 %copy.22 = f32[16,256]{1,0:T(8,128)} copy(f32[16,256]{1,0:T(8,128)} %get-tuple-element.18) | data formatting | bytes 32768
  84.3 1.3 %copy.23 = f32[16,256]{1,0:T(8,128)} copy(f32[16,256]{1,0:T(8,128)} %get-tuple-element.19) | data formatting | bytes 32768

commit v2 on v1

--- a/solution.py
+++ b/solution.py
@@ -38,17 +38,18 @@
     n_dp,
     n_ctx,
     group,
+    members,
+    wide_four,
     q_ref,
     k_ref,
     v_ref,
     og_ref,
     seg_row_ref,
-    seg_col_ref,
     f_ref,
     p_ref,
     m1_ref,
     m2_ref,
-    bias_ref,
+    step_ref,
     qg_ref,
     up_ref,
     m1_out,
@@ -60,16 +61,16 @@
     seg_all,
     kvacc,
     kv_in,
-    kv_pair,
+    kv_all,
     pall,
-    fcat,
+    f2,
+    f4,
     gacc,
     pp,
     cx,
     sb,
     rb,
-    dall,
-    dother,
+    dual,
     dfull,
     kvs_send,
     kvs_recv,
@@ -84,6 +85,10 @@
     red_recv,
     dir_send,
     dir_recv,
+    fwd_send,
+    fwd_recv,
+    mem_send,
+    mem_recv,
 ):
     tok = q_ref.shape[0]
     hd = k_ref.shape[1]
@@ -101,8 +106,11 @@
     lines = n_dp // 2
     mate = d + 1 - 2 * side
     slab = p_ref.shape[0]
-    half = slab // 2
+    wide_two = (slab - members * wide_four) // 2
     rows = m1_ref.shape[0]
+    spot = lax.rem(c, members)
+    base = c - spot
+    near = spot + 1 - 2 * core
 
     barrier = pltpu.get_barrier_semaphore()
 
@@ -126,16 +134,30 @@
             src_ref=src, dst_ref=dst, send_sem=send, recv_sem=recv, device_id=device, device_id_type=MESH
         )
 
-    def own_feature_copy(index):
-        return pltpu.make_async_copy(
-            f_ref.at[:, pl.ds(pl.multiple_of(index * slab + core * half, half), half)],
-            fcat.at[0, :, pl.ds(index * half, half)],
-            local_sem,
-        )
+    def two_at(index, of_core):
+        start = index * slab + members * wide_four + of_core * wide_two
+        return pl.ds(pl.multiple_of(start, 128), wide_two)
+
+    def four_at(index, of_spot):
+        return pl.ds(pl.multiple_of(index * slab + of_spot * wide_four, 128), wide_four)
+
+    def two_to(index):
+        return pl.ds(index * wide_two, wide_two)
+
+    def four_to(index):
+        return pl.ds(index * wide_four, wide_four)
 
     for index in range(n_dp):
-        own_feature_copy(index).start()
-    pall[d] = p_ref[pl.ds(pl.multiple_of(core * half, half), half), :]
+        pltpu.make_async_copy(
+            f_ref.at[:, two_at(index, core)], f2.at[0, :, two_to(index)], local_sem.at[0]
+        ).start()
+        if wide_four:
+            pltpu.make_async_copy(
+                f_ref.at[:, four_at(index, spot)], f4.at[spot, :, four_to(index)], local_sem.at[1]
+            ).start()
+    if wide_four:
+        pall[d, 0:wide_four, :] = p_ref[four_at(0, spot), :]
+    pall[d, wide_four : wide_four + wide_two, :] = p_ref[two_at(0, core), :]
     kall[c] = k_ref[...]
     vall[c] = v_ref[...]
     seg_all[c] = seg_row_ref[...]
@@ -170,26 +192,44 @@
     def _():
         p_copy(d, 1, d - 2).start()
 
-    def feature_copy(index):
+    def member(step):
+        return lax.rem(spot + step, members)
+
+    def four_copy(step, index):
         return remote(
-            f_ref.at[:, pl.ds(pl.multiple_of(index * slab + (1 - core) * half, half), half)],
-            fcat.at[1, :, pl.ds(index * half, half)],
+            f_ref.at[:, four_at(index, member(step))],
+            f4.at[spot, :, four_to(index)],
+            mem_send.at[0, step],
+            mem_recv.at[0, spot],
+            (d, base + member(step)),
+        )
+
+    if wide_four:
+        for index in range(n_dp):
+            for step in range(1, members):
+                four_copy(step, index).start()
+    for index in range(n_dp):
+        remote(
+            f_ref.at[:, two_at(index, 1 - core)],
+            f2.at[1, :, two_to(index)],
             one_send.at[0],
             one_recv.at[0],
             (d, other),
-        )
-
-    for index in range(n_dp):
-        feature_copy(index).start()
+        ).start()
 
     def p_arrived(index):
         p_copy(index, 2, mate).wait_recv()
 
     def project(index):
-        piece = pall[index]
-        cols = pl.ds(pl.multiple_of(index * half, half), half)
-        gacc[0] += dot_nn(fcat[0, :, cols], piece)
-        gacc[1] += dot_nn(fcat[1, :, cols], piece)
+        cols = pl.ds(pl.multiple_of(index * wide_two, 128), wide_two)
+        piece = pall[index, wide_four : wide_four + wide_two, :]
+        gacc[spot] += dot_nn(f2[0, :, cols], piece)
+        gacc[near] += dot_nn(f2[1, :, cols], piece)
+        if wide_four:
+            cols = pl.ds(pl.multiple_of(index * wide_four, 128), wide_four)
+            lhs = f4[:, :, cols].reshape(members * tok, wide_four)
+            out = dot_nn(lhs, pall[index, 0:wide_four, :])
+            gacc[...] += out.reshape(members, tok, out.shape[1])
 
     def forward(distance):
         src = line - distance
@@ -252,8 +292,14 @@
     width = group * tok
     starts = jnp.zeros((8, width), F32)
     ones = jnp.ones((8, tok), BF16)
+    turn = lax.broadcasted_iota(jnp.int32, (width, tok), 0) - lax.broadcasted_iota(
+        jnp.int32, (width, tok), 1
+    )
+    same = jnp.where(lax.rem(turn + tok, tok) == 0, 1.0, 0.0).astype(BF16)
+    own_row = jnp.broadcast_to(seg_row_ref[...], (8, tok)).astype(F32).astype(BF16)
+    own_col = dot_nt(same, own_row)[:, 0:1]
     for block in range(n_ctx):
-        below = jnp.where(seg_all[block] < seg_col_ref[...], 1.0, 0.0).astype(BF16)
+        below = jnp.where(seg_all[block].astype(F32) < own_col, 1.0, 0.0).astype(BF16)
         starts = starts + dot_nt(ones, below)
     first_key = starts[0:1, :].astype(jnp.int32)
     lane = lax.broadcasted_iota(jnp.int32, (1, width), 1)
@@ -302,8 +348,15 @@
     for step in range(1, n_ctx):
         kv_copy(step).start()
 
-    pltpu.make_async_copy(fcat.at[0], fcat.at[0], local_sem).wait()
-    remote(fcat.at[1], fcat.at[1], one_send.at[0], one_recv.at[0], (d, other)).wait_recv()
+    pltpu.make_async_copy(f2.at[0], f2.at[0], local_sem.at[0]).wait()
+    remote(f2.at[1], f2.at[1], one_send.at[0], one_recv.at[0], (d, other)).wait_recv()
+    if wide_four:
+        pltpu.make_async_copy(f4.at[spot], f4.at[spot], local_sem.at[1]).wait()
+        for step in range(1, members):
+            source = lax.rem(spot + members - step, members)
+            remote(
+                f4.at[source], f4.at[source], mem_send.at[0, step], mem_recv.at[0, source], (d, other)
+            ).wait_recv()
     gacc[...] = jnp.zeros_like(gacc)
     project(d)
     project_across(0)
@@ -319,11 +372,19 @@
             kv_in.at[source], kv_in.at[source], rs_send.at[step], rs_recv.at[source], (d, other)
         ).wait_recv()
         total = total + kv_in[source]
-    kv_pair[0] = total.astype(BF16)
-    kv_copy_pair = remote(
-        kv_pair.at[0], kv_pair.at[1], one_send.at[1], one_recv.at[1], (d, other)
-    )
-    kv_copy_pair.start()
+    kv_all[spot] = total.astype(BF16)
+
+    def kv_low_copy(step):
+        return remote(
+            kv_all.at[spot],
+            kv_all.at[spot],
+            mem_send.at[1, step],
+            mem_recv.at[1, spot],
+            (d, base + member(step)),
+        )
+
+    for step in range(1, members):
+        kv_low_copy(step).start()
 
     for distance in range(1, lines):
         if distance > 2:
@@ -331,13 +392,15 @@
         if distance > 1:
             project_line(distance)
         project_across(distance)
-    kv_copy_pair.wait()
-
-    term = jnp.zeros((gacc.shape[2], 2 * hd), F32)
-    for part in range(2):
-        high, low = split_two(gacc[part])
-        kv_now = kv_pair[part]
-        term = term + dot_tn(high, kv_now) + dot_tn(low, kv_now)
+    for step in range(1, members):
+        source = lax.rem(spot + members - step, members)
+        remote(
+            kv_all.at[source], kv_all.at[source], mem_send.at[1, step], mem_recv.at[1, source], (d, other)
+        ).wait_recv()
+
+    kv_flat = kv_all[...].reshape(members * tok, 2 * hd)
+    high, low = split_two(gacc[...].reshape(members * tok, gacc.shape[2]))
+    term = dot_tn(high, kv_flat) + dot_tn(low, kv_flat)
     for index in range(chips):
         for k in range(2):
             at = (index * 2 + k) * rows
@@ -369,48 +432,97 @@
     projected = jnp.sum(rb[...], axis=0)
     first_new = BETA_ONE * m1_ref[...] + (1.0 - BETA_ONE) * projected
     second_new = BETA_TWO * m2_ref[...] + (1.0 - BETA_TWO) * projected * projected
-    bias_first = bias_ref[0:1, 0:1]
-    bias_second = bias_ref[0:1, 1:2]
+    count = jnp.full((1, 2 * hd), step_ref[0], jnp.int32)
+
+    def one_less_power(beta):
+        power = jnp.ones((1, 2 * hd), F32)
+        square = jnp.full((1, 2 * hd), beta, F32)
+        for bit in range(31):
+            power = jnp.where((count >> bit) & 1 == 1, power * square, power)
+            square = square * square
+        return 1.0 - power
+
+    bias_first = one_less_power(BETA_ONE)
+    bias_second = one_less_power(BETA_TWO)
     m1_out[...] = first_new
     m2_out[...] = second_new
-    dall[chip] = first_new / bias_first / (jnp.sqrt(second_new / bias_second) + EPSILON)
+    direction = first_new / bias_first / (jnp.sqrt(second_new / bias_second) + EPSILON)
+    dual[core, chip] = direction.astype(dual.dtype)
 
     def dir_copy(step):
         to = lax.rem(chip + step, chips)
         return remote(
-            dall.at[chip], dall.at[chip], dir_send.at[step], dir_recv.at[chip], chip_device(to)
+            dual.at[core, chip],
+            dual.at[core, chip],
+            dir_send.at[step],
+            dir_recv.at[chip],
+            chip_device(to),
+        )
+
+    def dir_pass(index):
+        return remote(
+            dual.at[core, index],
+            dual.at[core, index],
+            fwd_send.at[index],
+            fwd_recv.at[index],
+            (d, other),
         )
 
     @pl.loop(1, chips)
     def _(step):
         dir_copy(step).start()
+
+    dir_pass(chip).start()
 
     @pl.loop(1, chips)
     def _(step):
         source = lax.rem(chip + chips - step, chips)
         remote(
-            dall.at[source], dall.at[source], dir_send.at[step], dir_recv.at[source], chip_device(source)
+            dual.at[core, source],
+            dual.at[core, source],
+            dir_send.at[step],
+            dir_recv.at[source],
+            chip_device(source),
         ).wait_recv()
-
-    swap_dir = remote(dall, dother, one_send.at[3], one_recv.at[3], (d, other))
-    swap_dir.start()
-    swap_dir.wait()
-    even = jnp.where(core == 0, dall[...], dother[...])
-    odd = jnp.where(core == 0, dother[...], dall[...])
+        dir_pass(source).start()
+
+    @pl.loop(0, chips)
+    def _(index):
+        remote(
+            dual.at[1 - core, index],
+            dual.at[1 - core, index],
+            fwd_send.at[index],
+            fwd_recv.at[index],
+            (d, other),
+        ).wait_recv()
+
     for index in range(chips):
         at = index * 2 * rows
-        dfull[at : at + rows, :] = even[index]
-        dfull[at + rows : at + 2 * rows, :] = odd[index]
-    high, low = split_two(dfull[...])
+        dfull[at : at + rows, :] = dual[0, index]
+        dfull[at + rows : at + 2 * rows, :] = dual[1, index]
     out_rows = up_ref.shape[0]
     p_rows = p_ref[pl.ds(pl.multiple_of(c * out_rows, out_rows), out_rows), :]
-    up_ref[...] = dot_nn(p_rows, high) + dot_nn(p_rows, low)
+    if dfull.dtype == BF16:
+        up_ref[...] = dot_nn(p_rows, dfull[...])
+    else:
+        high, low = split_two(dfull[...])
+        up_ref[...] = dot_nn(p_rows, high) + dot_nn(p_rows, low)
 
     for step in range(1, n_ctx):
         for copy in kvs_copies(step):
             copy.wait_send()
         kv_copy(step).wait_send()
-    remote(fcat.at[1], fcat.at[1], one_send.at[0], one_recv.at[0], (d, other)).wait_send()
+    remote(f2.at[1], f2.at[1], one_send.at[0], one_recv.at[0], (d, other)).wait_send()
+    for step in range(1, members):
+        kv_low_copy(step).wait_send()
+        if wide_four:
+            remote(
+                f4.at[0], f4.at[0], mem_send.at[0, step], mem_recv.at[0, 0], (d, other)
+            ).wait_send()
+
+    @pl.loop(0, chips)
+    def _(index):
+        dir_pass(index).wait_send()
 
     @pl.loop(1, chips)
     def _(step):
@@ -437,6 +549,15 @@
             @pl.when(line > 0)
             def _():
                 p_copy(back * 2 + side, 1, d - 2).wait_send()
+
+
+def hand_over(a, b, c, d, a_out, b_out, c_out, d_out, sems):
+    pairs = ((a, a_out), (b, b_out), (c, c_out), (d, d_out))
+    copies = [pltpu.make_async_copy(x, y, sems.at[i]) for i, (x, y) in enumerate(pairs)]
+    for copy in copies:
+        copy.start()
+    for copy in copies:
+        copy.wait()
 
 
 def shards(
@@ -458,28 +579,22 @@
     slab, rank = projector.shape
     rows, kvw = first_moment.shape
     chips = n_dp * n_ctx // 2
-    half = slab // 2
     group = 4 if n_ctx * tok <= 1024 else 1
-    step_count = adam_step[0].astype(F32)
-    bias = jnp.stack(
-        [
-            1.0 - jnp.power(F32(BETA_ONE), step_count),
-            1.0 - jnp.power(F32(BETA_TWO), step_count),
-        ]
-    ).reshape(1, 2)
-    seg_col = jnp.tile(segments.reshape(tok, 1), (group, 1))
+    members, wide_four = (4, slab // 8) if slab % 1024 == 0 and n_ctx % 4 == 0 else (2, 0)
+    wide_two = (slab - members * wide_four) // 2
+    dir_type = BF16 if rows % 16 == 0 else F32
     vmem = pl.BlockSpec(memory_space=pltpu.VMEM)
     hbm = pl.BlockSpec(memory_space=pl.ANY)
     dma = pltpu.SemaphoreType.DMA
-    query_grad, update, first_new, second_new = pl.pallas_call(
-        functools.partial(body, n_dp, n_ctx, group),
+    results = pl.pallas_call(
+        functools.partial(body, n_dp, n_ctx, group, members, wide_four),
         out_shape=(
             jax.ShapeDtypeStruct((tok, HEADS * hd), BF16),
             jax.ShapeDtypeStruct((width // (n_dp * n_ctx), kvw), F32),
             jax.ShapeDtypeStruct((rows, kvw), F32),
             jax.ShapeDtypeStruct((rows, kvw), F32),
         ),
-        in_specs=[vmem] * 6 + [hbm] + [vmem] * 4,
+        in_specs=[vmem] * 5 + [hbm] + [vmem] * 3 + [pl.BlockSpec(memory_space=pltpu.SMEM)],
         out_specs=[vmem] * 4,
         scratch_shapes=[
             pltpu.VMEM((HEADS * tok, hd), BF16),
@@ -489,17 +604,17 @@
             pltpu.VMEM((n_ctx, 1, tok), jnp.int32),
             pltpu.VMEM((n_ctx, tok, kvw), F32),
             pltpu.VMEM((n_ctx, tok, kvw), F32),
-            pltpu.VMEM((2, tok, kvw), BF16),
-            pltpu.VMEM((n_dp, half, rank), BF16),
-            pltpu.VMEM((2, tok, width // 2), BF16),
-            pltpu.VMEM((2, tok, rank), F32),
+            pltpu.VMEM((members, tok, kvw), BF16),
+            pltpu.VMEM((n_dp, wide_four + wide_two, rank), BF16),
+            pltpu.VMEM((2, tok, n_dp * wide_two), BF16),
+            pltpu.VMEM((members, tok, n_dp * max(wide_four, 128)), BF16),
+            pltpu.VMEM((members, tok, rank), F32),
             pltpu.VMEM((2, chips, rows, kvw), F32),
             pltpu.VMEM((chips, rows, kvw), F32),
             pltpu.VMEM((chips, rows, kvw), F32),
             pltpu.VMEM((chips, rows, kvw), F32),
-            pltpu.VMEM((chips, rows, kvw), F32),
-            pltpu.VMEM((chips, rows, kvw), F32),
-            pltpu.VMEM((rank, kvw), F32),
+            pltpu.VMEM((2, chips, rows, kvw), dir_type),
+            pltpu.VMEM((rank, kvw), dir_type),
             dma((3, n_ctx)),
             dma((3, n_ctx)),
             dma((n_ctx,)),
@@ -508,11 +623,15 @@
             dma((n_dp,)),
             dma((4,)),
             dma((4,)),
-            dma(()),
+            dma((2,)),
             dma((chips,)),
             dma((chips,)),
             dma((chips,)),
             dma((chips,)),
+            dma((chips,)),
+            dma((chips,)),
+            dma((2, members)),
+            dma((2, members)),
         ],
         compiler_params=pltpu.CompilerParams(
             collective_id=0, has_side_effects=True, vmem_limit_bytes=56 * 2**20
@@ -523,13 +642,20 @@
         values[0],
         out_grad[0],
         segments,
-        seg_col,
         features[0],
         projector,
         first_moment,
         second_moment,
-        bias,
+        adam_step,
     )
+    query_grad, update, first_new, second_new = pl.pallas_call(
+        hand_over,
+        out_shape=tuple(jax.ShapeDtypeStruct(r.shape, r.dtype) for r in results),
+        in_specs=[hbm] * 4,
+        out_specs=[hbm] * 4,
+        scratch_shapes=[dma((4,))],
+        compiler_params=pltpu.CompilerParams(vmem_limit_bytes=60 * 2**20),
+    )(*results)
     return (query_grad[None], update, first_new, second_new)
 
 

time: 86.1 us -> 105 us (1.22)
  Pallas kernels: 75.8 us -> 103 us
  local copies, waits for them, and re-layouts: 7.89 us -> 0 us
    pallas_call x1 -> x2, Pallas kernels: 75.8 us -> 103 us  [the longest x1 79 us: shards(): pl.pallas_call(functools.partial(body, n_dp, n_ctx, group, members, wide_...]
    unnamed x4 -> x0, local copies, waits for them, and re-layouts: 6.13 us -> none
    another operation x2 -> x0, local copies, waits for them, and re-layouts: 1.76 us -> none  [shards(): seg_col = jnp.tile(segments.reshape(tok, 1), (group, 1))]
where the time goes in v2:
time: 105 us; the launch traced here: 104 us
  Pallas kernels  103 us (98%)
  between operations  1.45 us (1%)
    pallas_call x1, Pallas kernels, shards(): pl.pallas_call(functools.partial(body, n_dp, n_ctx, group, members, wide_...  79 us
    pallas_call x1, Pallas kernels, shards(): pl.pallas_call(hand_over, out_shape=tuple((jax.ShapeDtypeStruct(r.shape,...  24 us

profile of v2, /device:TPU:1, one launch (start us, length us, event | category | flops | bytes accessed | tf_op | source)
XLA Modules:
  0.0 104.5 jit_solution(11027064958789793911)
XLA Ops:
  1.3 79.0 %shard_map.129 = (bf16[224,1024]{1,0:T(8,128)(2,1)}, f32[256,256]{1,0:T(8,128)}, f32[16,256]{1,0:T(8,128)}, f32[16,256]{1,0:T(8,128)}) custom-call(bf16[224,1024]{1,0:T(8,128)(2,1)} %bitcast.7, bf16[224,128]{1,0:T(8,128)(2,1)} %bitcast.9, bf16[224,128]{1,0:T(8,128)(2,1)} %bitcast.10, bf16[224,1024]{1,0:T(8,128)(2,1)} %bitcast.8, s32[1,224]{1,0:T(1,128)} %seg_row_ref.1, ...), custom_call_target="tpu_custom_call" | custom-call | tf_op jit(solution)/shard_map/pallas_call | solution.py:589
  80.3 24.0 %shard_map.130 = (bf16[224,1024]{1,0:T(8,128)(2,1)}, f32[256,256]{1,0:T(8,128)}, f32[16,256]{1,0:T(8,128)}, f32[16,256]{1,0:T(8,128)}) custom-call(bf16[224,1024]{1,0:T(8,128)(2,1)} %get-tuple-element.12.a, f32[256,256]{1,0:T(8,128)} %get-tuple-element.13.b, f32[16,256]{1,0:T(8,128)} %get-tuple-element.14.c, f32[16,256]{1,0:T(8,128)} %get-tuple-element.15.d), custom_call_target="tpu_custom_call" | custom-call | tf_op jit(solution)/shard_map/pallas_call | solution.py:651

commit v3 on v2

--- a/solution.py
+++ b/solution.py
@@ -61,6 +61,8 @@
     seg_all,
     kvacc,
     kv_in,
+    kv_sum,
+    kv_two,
     kv_all,
     pall,
     f2,
@@ -204,6 +206,78 @@
             (d, base + member(step)),
         )
 
+    def p_arrived(index):
+        p_copy(index, 2, mate).wait_recv()
+
+    def project(index):
+        cols = pl.ds(pl.multiple_of(index * wide_two, 128), wide_two)
+        piece = pall[index, wide_four : wide_four + wide_two, :]
+        gacc[spot] += dot_nn(f2[0, :, cols], piece)
+        gacc[near] += dot_nn(f2[1, :, cols], piece)
+        if wide_four:
+            cols = pl.ds(pl.multiple_of(index * wide_four, 128), wide_four)
+            lhs = f4[:, :, cols].reshape(members * tok, wide_four)
+            out = dot_nn(lhs, pall[index, 0:wide_four, :])
+            gacc[...] += out.reshape(members, tok, out.shape[1])
+
+    def forward(distance):
+        src = line - distance
+
+        @pl.when(src >= 0)
+        def _():
+            index = src * 2 + side
+            p_arrived(index)
+
+            @pl.when(line + 1 < lines)
+            def _():
+                p_copy(index, 0, d + 2).start()
+
+            p_copy(index, 2, mate).start()
+
+        back = line + distance
+
+        @pl.when(back < lines)
+        def _():
+            index = back * 2 + side
+            p_arrived(index)
+
+            @pl.when(line > 0)
+            def _():
+                p_copy(index, 1, d - 2).start()
+
+            p_copy(index, 2, mate).start()
+
+    def project_line(distance):
+        @pl.when(line - distance >= 0)
+        def _():
+            project((line - distance) * 2 + side)
+
+        @pl.when(line + distance < lines)
+        def _():
+            project((line + distance) * 2 + side)
+
+    def project_across(distance):
+        @pl.when(line - distance >= 0)
+        def _():
+            index = (line - distance) * 2 + 1 - side
+            p_arrived(index)
+            project(index)
+
+        if distance > 0:
+
+            @pl.when(line + distance < lines)
+            def _():
+                index = (line + distance) * 2 + 1 - side
+                p_arrived(index)
+                project(index)
+
+    for step in range(1, n_ctx):
+        source = lax.rem(c + n_ctx - step, n_ctx)
+        for i, buf in enumerate((seg_all, kall, vall)):
+            remote(
+                buf.at[source], buf.at[source], kvs_send.at[i, step], kvs_recv.at[i, source], (d, other)
+            ).wait_recv()
+
     if wide_four:
         for index in range(n_dp):
             for step in range(1, members):
@@ -216,78 +290,6 @@
             one_recv.at[0],
             (d, other),
         ).start()
-
-    def p_arrived(index):
-        p_copy(index, 2, mate).wait_recv()
-
-    def project(index):
-        cols = pl.ds(pl.multiple_of(index * wide_two, 128), wide_two)
-        piece = pall[index, wide_four : wide_four + wide_two, :]
-        gacc[spot] += dot_nn(f2[0, :, cols], piece)
-        gacc[near] += dot_nn(f2[1, :, cols], piece)
-        if wide_four:
-            cols = pl.ds(pl.multiple_of(index * wide_four, 128), wide_four)
-            lhs = f4[:, :, cols].reshape(members * tok, wide_four)
-            out = dot_nn(lhs, pall[index, 0:wide_four, :])
-            gacc[...] += out.reshape(members, tok, out.shape[1])
-
-    def forward(distance):
-        src = line - distance
-
-        @pl.when(src >= 0)
-        def _():
-            index = src * 2 + side
-            p_arrived(index)
-
-            @pl.when(line + 1 < lines)
-            def _():
-                p_copy(index, 0, d + 2).start()
-
-            p_copy(index, 2, mate).start()
-
-        back = line + distance
-
-        @pl.when(back < lines)
-        def _():
-            index = back * 2 + side
-            p_arrived(index)
-
-            @pl.when(line > 0)
-            def _():
-                p_copy(index, 1, d - 2).start()
-
-            p_copy(index, 2, mate).start()
-
-    def project_line(distance):
-        @pl.when(line - distance >= 0)
-        def _():
-            project((line - distance) * 2 + side)
-
-        @pl.when(line + distance < lines)
-        def _():
-            project((line + distance) * 2 + side)
-
-    def project_across(distance):
-        @pl.when(line - distance >= 0)
-        def _():
-            index = (line - distance) * 2 + 1 - side
-            p_arrived(index)
-            project(index)
-
-        if distance > 0:
-
-            @pl.when(line + distance < lines)
-            def _():
-                index = (line + distance) * 2 + 1 - side
-                p_arrived(index)
-                project(index)
-
-    for step in range(1, n_ctx):
-        source = lax.rem(c + n_ctx - step, n_ctx)
-        for i, buf in enumerate((seg_all, kall, vall)):
-            remote(
-                buf.at[source], buf.at[source], kvs_send.at[i, step], kvs_recv.at[i, source], (d, other)
-            ).wait_recv()
 
     width = group * tok
     starts = jnp.zeros((8, width), F32)
@@ -340,14 +342,24 @@
         attend(index)
         if index == 0 and lines > 1:
             forward(1)
+        if index == groups - 2 and lines > 2:
+            forward(2)
+
+    def core_copy(index):
+        return remote(
+            kvacc.at[index * 2 + 1 - core], kv_in.at[index], rs_send.at[0, index], rs_recv.at[0, index], (d, other)
+        )
+
+    place = c // 2
 
     def kv_copy(step):
-        to = lax.rem(c + step, n_ctx)
-        return remote(kvacc.at[to], kv_in.at[c], rs_send.at[step], rs_recv.at[c], (d, to))
-
-    for step in range(1, n_ctx):
-        kv_copy(step).start()
-
+        to = lax.rem(place + step, half_ctx)
+        return remote(
+            kv_sum.at[to], kv_two.at[place], rs_send.at[1, step], rs_recv.at[1, place], (d, to * 2 + core)
+        )
+
+    for index in range(half_ctx):
+        core_copy(index).start()
     pltpu.make_async_copy(f2.at[0], f2.at[0], local_sem.at[0]).wait()
     remote(f2.at[1], f2.at[1], one_send.at[0], one_recv.at[0], (d, other)).wait_recv()
     if wide_four:
@@ -358,20 +370,25 @@
                 f4.at[source], f4.at[source], mem_send.at[0, step], mem_recv.at[0, source], (d, other)
             ).wait_recv()
     gacc[...] = jnp.zeros_like(gacc)
+    for index in range(half_ctx):
+        core_copy(index).wait_recv()
+        kv_sum[index] = kvacc[index * 2 + core] + kv_in[index]
+    for step in range(1, half_ctx):
+        kv_copy(step).start()
     project(d)
     project_across(0)
     if lines > 1:
         project_line(1)
-    if lines > 2:
-        forward(2)
-
-    total = kvacc[c]
-    for step in range(1, n_ctx):
-        source = lax.rem(c + n_ctx - step, n_ctx)
+    if lines > 3:
+        forward(3)
+
+    total = kv_sum[place]
+    for step in range(1, half_ctx):
+        source = lax.rem(place + half_ctx - step, half_ctx)
         remote(
-            kv_in.at[source], kv_in.at[source], rs_send.at[step], rs_recv.at[source], (d, other)
+            kv_two.at[source], kv_two.at[source], rs_send.at[1, step], rs_recv.at[1, source], (d, other)
         ).wait_recv()
-        total = total + kv_in[source]
+        total = total + kv_two[source]
     kv_all[spot] = total.astype(BF16)
 
     def kv_low_copy(step):
@@ -387,7 +404,7 @@
         kv_low_copy(step).start()
 
     for distance in range(1, lines):
-        if distance > 2:
+        if distance > 3:
             forward(distance)
         if distance > 1:
             project_line(distance)
@@ -511,7 +528,10 @@
     for step in range(1, n_ctx):
         for copy in kvs_copies(step):
             copy.wait_send()
+    for step in range(1, half_ctx):
         kv_copy(step).wait_send()
+    for index in range(half_ctx):
+        core_copy(index).wait_send()
     remote(f2.at[1], f2.at[1], one_send.at[0], one_recv.at[0], (d, other)).wait_send()
     for step in range(1, members):
         kv_low_copy(step).wait_send()
@@ -551,12 +571,16 @@
                 p_copy(back * 2 + side, 1, d - 2).wait_send()
 
 
-def hand_over(a, b, c, d, a_out, b_out, c_out, d_out, sems):
-    pairs = ((a, a_out), (b, b_out), (c, c_out), (d, d_out))
-    copies = [pltpu.make_async_copy(x, y, sems.at[i]) for i, (x, y) in enumerate(pairs)]
-    for copy in copies:
+def hand_over(*refs):
+    ins, outs, held, sems = refs[0:4], refs[4:8], refs[8:12], refs[12]
+    load = [pltpu.make_async_copy(x, y, sems.at[0, i]) for i, (x, y) in enumerate(zip(ins, held))]
+    store = [pltpu.make_async_copy(x, y, sems.at[1, i]) for i, (x, y) in enumerate(zip(held, outs))]
+    for copy in load:
         copy.start()
-    for copy in copies:
+    for first, then in zip(load, store):
+        first.wait()
+        then.start()
+    for copy in store:
         copy.wait()
 
 
@@ -579,7 +603,7 @@
     slab, rank = projector.shape
     rows, kvw = first_moment.shape
     chips = n_dp * n_ctx // 2
-    group = 4 if n_ctx * tok <= 1024 else 1
+    group = 2 if n_ctx * tok <= 1024 else 1
     members, wide_four = (4, slab // 8) if slab % 1024 == 0 and n_ctx % 4 == 0 else (2, 0)
     wide_two = (slab - members * wide_four) // 2
     dir_type = BF16 if rows % 16 == 0 else F32
@@ -603,7 +627,9 @@
             pltpu.VMEM((n_ctx, tok, hd), BF16),
             pltpu.VMEM((n_ctx, 1, tok), jnp.int32),
             pltpu.VMEM((n_ctx, tok, kvw), F32),
-            pltpu.VMEM((n_ctx, tok, kvw), F32),
+            pltpu.VMEM((n_ctx // 2, tok, kvw), F32),
+            pltpu.VMEM((n_ctx // 2, tok, kvw), F32),
+            pltpu.VMEM((n_ctx // 2, tok, kvw), F32),
             pltpu.VMEM((members, tok, kvw), BF16),
             pltpu.VMEM((n_dp, wide_four + wide_two, rank), BF16),
             pltpu.VMEM((2, tok, n_dp * wide_two), BF16),
@@ -617,8 +643,8 @@
             pltpu.VMEM((rank, kvw), dir_type),
             dma((3, n_ctx)),
             dma((3, n_ctx)),
-            dma((n_ctx,)),
-            dma((n_ctx,)),
+            dma((2, n_ctx // 2)),
+            dma((2, n_ctx // 2)),
             dma((3, n_dp)),
             dma((n_dp,)),
             dma((4,)),
@@ -653,7 +679,7 @@
         out_shape=tuple(jax.ShapeDtypeStruct(r.shape, r.dtype) for r in results),
         in_specs=[hbm] * 4,
         out_specs=[hbm] * 4,
-        scratch_shapes=[dma((4,))],
+        scratch_shapes=[pltpu.VMEM(r.shape, r.dtype) for r in results] + [dma((2, 4))],
         compiler_params=pltpu.CompilerParams(vmem_limit_bytes=60 * 2**20),
     )(*results)
     return (query_grad[None], update, first_new, second_new)

time: 105 us -> 72.5 us (0.69)
  Pallas kernels: 103 us -> 70.9 us
    pallas_call x1, Pallas kernels: 24 us -> 1.95 us  [shards(): pl.pallas_call(hand_over, out_shape=tuple((jax.ShapeDtypeStruct(r.shape,...]
    pallas_call x1, Pallas kernels: 79 us -> 68.9 us  [shards(): pl.pallas_call(functools.partial(body, n_dp, n_ctx, group, members, wide_...]
where the time goes in v3:
time: 72.5 us; the launch traced here: 72.3 us
  Pallas kernels  70.9 us (98%)
  between operations  1.45 us (2%)
    pallas_call x1, Pallas kernels, shards(): pl.pallas_call(functools.partial(body, n_dp, n_ctx, group, members, wide_...  68.9 us
    pallas_call x1, Pallas kernels, shards(): pl.pallas_call(hand_over, out_shape=tuple((jax.ShapeDtypeStruct(r.shape,...  1.95 us

profile of v3, /device:TPU:1, one launch (start us, length us, event | category | flops | bytes accessed | tf_op | source)
XLA Modules:
  0.0 72.3 jit_solution(12332206799760138532)
XLA Ops:
  1.3 68.9 %shard_map.129 = (bf16[224,1024]{1,0:T(8,128)(2,1)}, f32[256,256]{1,0:T(8,128)}, f32[16,256]{1,0:T(8,128)}, f32[16,256]{1,0:T(8,128)}) custom-call(bf16[224,1024]{1,0:T(8,128)(2,1)} %bitcast.7, bf16[224,128]{1,0:T(8,128)(2,1)} %bitcast.9, bf16[224,128]{1,0:T(8,128)(2,1)} %bitcast.10, bf16[224,1024]{1,0:T(8,128)(2,1)} %bitcast.8, s32[1,224]{1,0:T(1,128)} %seg_row_ref.1, ...), custom_call_target="tpu_custom_call" | custom-call | tf_op jit(solution)/shard_map/pallas_call | solution.py:613
  70.2 1.9 %shard_map.130 = (bf16[224,1024]{1,0:T(8,128)(2,1)}, f32[256,256]{1,0:T(8,128)}, f32[16,256]{1,0:T(8,128)}, f32[16,256]{1,0:T(8,128)}) custom-call(bf16[224,1024]{1,0:T(8,128)(2,1)} %get-tuple-element.12.refs_0_, f32[256,256]{1,0:T(8,128)} %get-tuple-element.13.refs_1_, f32[16,256]{1,0:T(8,128)} %get-tuple-element.14.refs_2_, ...), custom_call_target="tpu_custom_call" | custom-call | tf_op jit(solution)/shard_map/pallas_call | solution.py:677

commit v4 on v3

--- a/solution.py
+++ b/solution.py
@@ -74,6 +74,8 @@
     rb,
     dual,
     dfull,
+    p_own,
+    bias,
     kvs_send,
     kvs_recv,
     rs_send,
@@ -93,6 +95,7 @@
     mem_recv,
 ):
     tok = q_ref.shape[0]
+    out_rows = up_ref.shape[0]
     hd = k_ref.shape[1]
     seq = n_ctx * tok
     scale = 1.0 / math.sqrt(hd)
@@ -158,14 +161,24 @@
                 f_ref.at[:, four_at(index, spot)], f4.at[spot, :, four_to(index)], local_sem.at[1]
             ).start()
     if wide_four:
-        pall[d, 0:wide_four, :] = p_ref[four_at(0, spot), :]
-    pall[d, wide_four : wide_four + wide_two, :] = p_ref[two_at(0, core), :]
-    kall[c] = k_ref[...]
-    vall[c] = v_ref[...]
+        pltpu.make_async_copy(
+            p_ref.at[four_at(0, spot), :], pall.at[d, pl.ds(0, wide_four), :], local_sem.at[6]
+        ).start()
+    pltpu.make_async_copy(
+        p_ref.at[two_at(0, core), :], pall.at[d, pl.ds(wide_four, wide_two), :], local_sem.at[6]
+    ).start()
     seg_all[c] = seg_row_ref[...]
+    pltpu.make_async_copy(k_ref, kall.at[c], local_sem.at[4]).start()
+    pltpu.make_async_copy(v_ref, vall.at[c], local_sem.at[5]).start()
     for head in range(HEADS):
-        qs[head * tok : (head + 1) * tok, :] = q_ref[:, head * hd : (head + 1) * hd]
-        gs[head * tok : (head + 1) * tok, :] = og_ref[:, head * hd : (head + 1) * hd]
+        for i, (wide, packed) in enumerate(((q_ref, qs), (og_ref, gs))):
+            pltpu.make_async_copy(
+                wide.at[:, pl.ds(head * hd, hd)], packed.at[pl.ds(head * tok, tok), :], local_sem.at[2 + i]
+            ).start()
+    p_rows_copy = pltpu.make_async_copy(
+        p_ref.at[pl.ds(pl.multiple_of(c * out_rows, out_rows), out_rows), :], p_own, local_sem.at[7]
+    )
+    p_rows_copy.start()
     pl.semaphore_wait(barrier, chips - 1 + half_ctx)
 
     def kvs_copies(step):
@@ -175,24 +188,39 @@
             for i, buf in enumerate((seg_all, kall, vall))
         ]
 
+    pltpu.make_async_copy(k_ref, kall.at[c], local_sem.at[4]).wait()
+    pltpu.make_async_copy(v_ref, vall.at[c], local_sem.at[5]).wait()
+
     for step in range(1, n_ctx):
         for copy in kvs_copies(step):
             copy.start()
 
-    def p_copy(index, way, device_dp):
+    chunk_rows = (wide_four + wide_two) // 2
+
+    def p_copy(index, way, device_dp, chunk):
+        piece = pall.at[index, pl.ds(chunk * chunk_rows, chunk_rows), :]
         return remote(
-            pall.at[index], pall.at[index], p_send.at[way, index], p_recv.at[index], (device_dp, c)
-        )
-
-    p_copy(d, 2, mate).start()
-
-    @pl.when(line + 1 < lines)
-    def _():
-        p_copy(d, 0, d + 2).start()
-
-    @pl.when(line > 0)
-    def _():
-        p_copy(d, 1, d - 2).start()
+            piece, piece, p_send.at[way, index, chunk], p_recv.at[index, chunk], (device_dp, c)
+        )
+
+    def pass_on(index, chunk, right, left):
+        if right:
+
+            @pl.when(line + 1 < lines)
+            def _():
+                p_copy(index, 0, d + 2, chunk).start()
+
+        if left:
+
+            @pl.when(line > 0)
+            def _():
+                p_copy(index, 1, d - 2, chunk).start()
+
+        p_copy(index, 2, mate, chunk).start()
+
+    pltpu.make_async_copy(pall.at[d], pall.at[d], local_sem.at[6]).wait()
+    for chunk in range(2):
+        pass_on(d, chunk, True, True)
 
     def member(step):
         return lax.rem(spot + step, members)
@@ -206,8 +234,8 @@
             (d, base + member(step)),
         )
 
-    def p_arrived(index):
-        p_copy(index, 2, mate).wait_recv()
+    def p_arrived(index, chunk):
+        p_copy(index, 2, mate, chunk).wait_recv()
 
     def project(index):
         cols = pl.ds(pl.multiple_of(index * wide_two, 128), wide_two)
@@ -222,30 +250,18 @@
 
     def forward(distance):
         src = line - distance
-
-        @pl.when(src >= 0)
-        def _():
-            index = src * 2 + side
-            p_arrived(index)
-
-            @pl.when(line + 1 < lines)
+        back = line + distance
+        for chunk in range(2):
+
+            @pl.when(src >= 0)
             def _():
-                p_copy(index, 0, d + 2).start()
-
-            p_copy(index, 2, mate).start()
-
-        back = line + distance
-
-        @pl.when(back < lines)
-        def _():
-            index = back * 2 + side
-            p_arrived(index)
-
-            @pl.when(line > 0)
+                p_arrived(src * 2 + side, chunk)
+                pass_on(src * 2 + side, chunk, True, False)
+
+            @pl.when(back < lines)
             def _():
-                p_copy(index, 1, d - 2).start()
-
-            p_copy(index, 2, mate).start()
+                p_arrived(back * 2 + side, chunk)
+                pass_on(back * 2 + side, chunk, False, True)
 
     def project_line(distance):
         @pl.when(line - distance >= 0)
@@ -260,7 +276,8 @@
         @pl.when(line - distance >= 0)
         def _():
             index = (line - distance) * 2 + 1 - side
-            p_arrived(index)
+            p_arrived(index, 0)
+            p_arrived(index, 1)
             project(index)
 
         if distance > 0:
@@ -268,7 +285,8 @@
             @pl.when(line + distance < lines)
             def _():
                 index = (line + distance) * 2 + 1 - side
-                p_arrived(index)
+                p_arrived(index, 0)
+                p_arrived(index, 1)
                 project(index)
 
     for step in range(1, n_ctx):
@@ -308,16 +326,19 @@
     query_pos = c * tok + lax.rem(lane, tok)
     key_pos = lax.broadcasted_iota(jnp.int32, (seq, width), 0)
 
+    bias[...] = jnp.where((key_pos <= query_pos) & (key_pos >= first_key), 0.0, -1e30)
+    pltpu.make_async_copy(qs, qs, local_sem.at[2]).wait()
+    pltpu.make_async_copy(gs, gs, local_sem.at[3]).wait()
+
     def attend(index):
         at = index * group * tok
         keys = kall[...].reshape(seq, hd)
         vals = vall[...].reshape(seq, hd)
         q_now = qs[at : at + width, :]
         g_now = gs[at : at + width, :]
-        allowed = (key_pos <= query_pos) & (key_pos >= first_key)
-        scores = jnp.where(allowed, dot_nt(keys, q_now) * scale, -1e30)
+        scores = dot_nt(keys, q_now) * (scale * math.log2(math.e)) + bias[...]
         top = jnp.max(scores, axis=0, keepdims=True)
-        expo = jnp.exp(scores - top)
+        expo = jnp.exp2(scores - top)
         inverse = 1.0 / jnp.sum(expo, axis=0, keepdims=True)
         dprob = dot_nt(vals, g_now)
         probs = expo * inverse
@@ -517,8 +538,8 @@
         at = index * 2 * rows
         dfull[at : at + rows, :] = dual[0, index]
         dfull[at + rows : at + 2 * rows, :] = dual[1, index]
-    out_rows = up_ref.shape[0]
-    p_rows = p_ref[pl.ds(pl.multiple_of(c * out_rows, out_rows), out_rows), :]
+    p_rows_copy.wait()
+    p_rows = p_own[...]
     if dfull.dtype == BF16:
         up_ref[...] = dot_nn(p_rows, dfull[...])
     else:
@@ -549,26 +570,31 @@
         sum_copy(step).wait_send()
         dir_copy(step).wait_send()
 
-    for distance in range(lines):
-        src = line - distance
-        back = line + distance
-
-        @pl.when(src >= 0)
+    def sent(index, right, left):
+        for chunk in range(2):
+            p_copy(index, 2, mate, chunk).wait_send()
+            if right:
+
+                @pl.when(line + 1 < lines)
+                def _():
+                    p_copy(index, 0, d + 2, chunk).wait_send()
+
+            if left:
+
+                @pl.when(line > 0)
+                def _():
+                    p_copy(index, 1, d - 2, chunk).wait_send()
+
+    sent(d, True, True)
+    for distance in range(1, lines):
+
+        @pl.when(line - distance >= 0)
         def _():
-            p_copy(src * 2 + side, 2, mate).wait_send()
-
-            @pl.when(line + 1 < lines)
-            def _():
-                p_copy(src * 2 + side, 0, d + 2).wait_send()
-
-        @pl.when(back < lines)
+            sent((line - distance) * 2 + side, True, False)
+
+        @pl.when(line + distance < lines)
         def _():
-            if distance > 0:
-                p_copy(back * 2 + side, 2, mate).wait_send()
-
-            @pl.when(line > 0)
-            def _():
-                p_copy(back * 2 + side, 1, d - 2).wait_send()
+            sent((line + distance) * 2 + side, False, True)
 
 
 def hand_over(*refs):
@@ -618,7 +644,7 @@
             jax.ShapeDtypeStruct((rows, kvw), F32),
             jax.ShapeDtypeStruct((rows, kvw), F32),
         ),
-        in_specs=[vmem] * 5 + [hbm] + [vmem] * 3 + [pl.BlockSpec(memory_space=pltpu.SMEM)],
+        in_specs=[hbm] * 4 + [vmem] + [hbm] * 2 + [vmem] * 2 + [pl.BlockSpec(memory_space=pltpu.SMEM)],
         out_specs=[vmem] * 4,
         scratch_shapes=[
             pltpu.VMEM((HEADS * tok, hd), BF16),
@@ -641,15 +667,17 @@
             pltpu.VMEM((chips, rows, kvw), F32),
             pltpu.VMEM((2, chips, rows, kvw), dir_type),
             pltpu.VMEM((rank, kvw), dir_type),
+            pltpu.VMEM((slab // n_ctx, rank), BF16),
+            pltpu.VMEM((n_ctx * tok, group * tok), F32),
             dma((3, n_ctx)),
             dma((3, n_ctx)),
             dma((2, n_ctx // 2)),
             dma((2, n_ctx // 2)),
-            dma((3, n_dp)),
-            dma((n_dp,)),
+            dma((3, n_dp, 2)),
+            dma((n_dp, 2)),
             dma((4,)),
             dma((4,)),
-            dma((2,)),
+            dma((8,)),
             dma((chips,)),
             dma((chips,)),
             dma((chips,)),

time: 72.5 us -> 72.2 us (level)
  no operation moved by 1% of the time
where the time goes in v4:
time: 72.2 us; the launch traced here: 71.9 us
  Pallas kernels  70.4 us (98%)
  between operations  1.45 us (2%)
    pallas_call x1, Pallas kernels, shards(): pl.pallas_call(functools.partial(body, n_dp, n_ctx, group, members, wide_...  68.5 us
    pallas_call x1, Pallas kernels, shards(): pl.pallas_call(hand_over, out_shape=tuple((jax.ShapeDtypeStruct(r.shape,...  1.95 us

profile of v4, /device:TPU:1, one launch (start us, length us, event | category | flops | bytes accessed | tf_op | source)
XLA Modules:
  0.0 71.9 jit_solution(9516006359099158680)
XLA Ops:
  1.3 68.5 %shard_map.129 = (bf16[224,1024]{1,0:T(8,128)(2,1)}, f32[256,256]{1,0:T(8,128)}, f32[16,256]{1,0:T(8,128)}, f32[16,256]{1,0:T(8,128)}) custom-call(bf16[224,1024]{1,0:T(8,128)(2,1)} %bitcast.7, bf16[224,128]{1,0:T(8,128)(2,1)} %bitcast.9, bf16[224,128]{1,0:T(8,128)(2,1)} %bitcast.10, bf16[224,1024]{1,0:T(8,128)(2,1)} %bitcast.8, s32[1,224]{1,0:T(1,128)} %seg_row_ref.1, ...), custom_call_target="tpu_custom_call" | custom-call | tf_op jit(solution)/shard_map/pallas_call | solution.py:639
  69.8 1.9 %shard_map.130 = (bf16[224,1024]{1,0:T(8,128)(2,1)}, f32[256,256]{1,0:T(8,128)}, f32[16,256]{1,0:T(8,128)}, f32[16,256]{1,0:T(8,128)}) custom-call(bf16[224,1024]{1,0:T(8,128)(2,1)} %get-tuple-element.12.refs_0_, f32[256,256]{1,0:T(8,128)} %get-tuple-element.13.refs_1_, f32[16,256]{1,0:T(8,128)} %get-tuple-element.14.refs_2_, ...), custom_call_target="tpu_custom_call" | custom-call | tf_op jit(solution)/shard_map/pallas_call | solution.py:705

commit v5 on v4

--- a/solution.py
+++ b/solution.py
@@ -181,19 +181,28 @@
     p_rows_copy.start()
     pl.semaphore_wait(barrier, chips - 1 + half_ctx)
 
-    def kvs_copies(step):
-        to = lax.rem(c + step, n_ctx)
+    place = c // 2
+
+    def peer(step):
+        return lax.rem(place + step, half_ctx) * 2 + core
+
+    def source_of(step):
+        return lax.rem(place + half_ctx - step, half_ctx) * 2 + core
+
+    def kvs_copies(slot, to, sem):
         return [
-            remote(buf.at[c], buf.at[c], kvs_send.at[i, step], kvs_recv.at[i, c], (d, to))
+            remote(buf.at[slot], buf.at[slot], kvs_send.at[i, sem], kvs_recv.at[i, slot], (d, to))
             for i, buf in enumerate((seg_all, kall, vall))
         ]
 
     pltpu.make_async_copy(k_ref, kall.at[c], local_sem.at[4]).wait()
     pltpu.make_async_copy(v_ref, vall.at[c], local_sem.at[5]).wait()
 
-    for step in range(1, n_ctx):
-        for copy in kvs_copies(step):
+    for step in range(1, half_ctx):
+        for copy in kvs_copies(c, peer(step), step):
             copy.start()
+    for copy in kvs_copies(c, other, 0):
+        copy.start()
 
     chunk_rows = (wide_four + wide_two) // 2
 
@@ -289,13 +298,13 @@
                 p_arrived(index, 1)
                 project(index)
 
-    for step in range(1, n_ctx):
-        source = lax.rem(c + n_ctx - step, n_ctx)
-        for i, buf in enumerate((seg_all, kall, vall)):
-            remote(
-                buf.at[source], buf.at[source], kvs_send.at[i, step], kvs_recv.at[i, source], (d, other)
-            ).wait_recv()
-
+    for step in range(1, half_ctx):
+        source = source_of(step)
+        for landed, onward in zip(
+            kvs_copies(source, other, step), kvs_copies(source, other, half_ctx + step)
+        ):
+            landed.wait_recv()
+            onward.start()
     if wide_four:
         for index in range(n_dp):
             for step in range(1, members):
@@ -308,6 +317,10 @@
             one_recv.at[0],
             (d, other),
         ).start()
+
+    for step in range(half_ctx):
+        for copy in kvs_copies(lax.rem(place + step, half_ctx) * 2 + 1 - core, other, 0):
+            copy.wait_recv()
 
     width = group * tok
     starts = jnp.zeros((8, width), F32)
@@ -371,8 +384,6 @@
             kvacc.at[index * 2 + 1 - core], kv_in.at[index], rs_send.at[0, index], rs_recv.at[0, index], (d, other)
         )
 
-    place = c // 2
-
     def kv_copy(step):
         to = lax.rem(place + step, half_ctx)
         return remote(
@@ -381,6 +392,11 @@
 
     for index in range(half_ctx):
         core_copy(index).start()
+    for index in range(half_ctx):
+        core_copy(index).wait_recv()
+        kv_sum[index] = kvacc[index * 2 + core] + kv_in[index]
+    for step in range(1, half_ctx):
+        kv_copy(step).start()
     pltpu.make_async_copy(f2.at[0], f2.at[0], local_sem.at[0]).wait()
     remote(f2.at[1], f2.at[1], one_send.at[0], one_recv.at[0], (d, other)).wait_recv()
     if wide_four:
@@ -391,11 +407,6 @@
                 f4.at[source], f4.at[source], mem_send.at[0, step], mem_recv.at[0, source], (d, other)
             ).wait_recv()
     gacc[...] = jnp.zeros_like(gacc)
-    for index in range(half_ctx):
-        core_copy(index).wait_recv()
-        kv_sum[index] = kvacc[index * 2 + core] + kv_in[index]
-    for step in range(1, half_ctx):
-        kv_copy(step).start()
     project(d)
     project_across(0)
     if lines > 1:
@@ -412,17 +423,20 @@
         total = total + kv_two[source]
     kv_all[spot] = total.astype(BF16)
 
-    def kv_low_copy(step):
+    far = lax.rem(spot + 2, members)
+
+    def kv_low_copy(slot, to, sem):
         return remote(
-            kv_all.at[spot],
-            kv_all.at[spot],
-            mem_send.at[1, step],
-            mem_recv.at[1, spot],
-            (d, base + member(step)),
-        )
-
-    for step in range(1, members):
-        kv_low_copy(step).start()
+            kv_all.at[slot],
+            kv_all.at[slot],
+            mem_send.at[1, sem],
+            mem_recv.at[1, slot],
+            (d, base + to),
+        )
+
+    if members == 4:
+        kv_low_copy(spot, far, 1).start()
+    kv_low_copy(spot, near, 0).start()
 
     for distance in range(1, lines):
         if distance > 3:
@@ -430,11 +444,11 @@
         if distance > 1:
             project_line(distance)
         project_across(distance)
-    for step in range(1, members):
-        source = lax.rem(spot + members - step, members)
-        remote(
-            kv_all.at[source], kv_all.at[source], mem_send.at[1, step], mem_recv.at[1, source], (d, other)
-        ).wait_recv()
+    if members == 4:
+        kv_low_copy(far, near, 2).wait_recv()
+        kv_low_copy(far, near, 2).start()
+        kv_low_copy(lax.rem(near + 2, members), near, 2).wait_recv()
+    kv_low_copy(near, near, 0).wait_recv()
 
     kv_flat = kv_all[...].reshape(members * tok, 2 * hd)
     high, low = split_two(gacc[...].reshape(members * tok, gacc.shape[2]))
@@ -546,16 +560,19 @@
         high, low = split_two(dfull[...])
         up_ref[...] = dot_nn(p_rows, high) + dot_nn(p_rows, low)
 
-    for step in range(1, n_ctx):
-        for copy in kvs_copies(step):
+    for step in range(half_ctx):
+        for copy in kvs_copies(c, other, step):
             copy.wait_send()
+        if step > 0:
+            for copy in kvs_copies(c, other, half_ctx + step):
+                copy.wait_send()
     for step in range(1, half_ctx):
         kv_copy(step).wait_send()
     for index in range(half_ctx):
         core_copy(index).wait_send()
     remote(f2.at[1], f2.at[1], one_send.at[0], one_recv.at[0], (d, other)).wait_send()
     for step in range(1, members):
-        kv_low_copy(step).wait_send()
+        kv_low_copy(spot, near, step - 1).wait_send()
         if wide_four:
             remote(
                 f4.at[0], f4.at[0], mem_send.at[0, step], mem_recv.at[0, 0], (d, other)

time: 72.2 us -> 69.3 us (0.960)
  Pallas kernels: 70.4 us -> 67.5 us
    pallas_call x1, Pallas kernels: 68.5 us -> 65.6 us  [shards(): pl.pallas_call(functools.partial(body, n_dp, n_ctx, group, members, wide_...]
where the time goes in v5:
time: 69.3 us; the launch traced here: 69 us
  Pallas kernels  67.5 us (97%)
  between operations  1.45 us (2%)
    pallas_call x1, Pallas kernels, shards(): pl.pallas_call(functools.partial(body, n_dp, n_ctx, group, members, wide_...  65.6 us
    pallas_call x1, Pallas kernels, shards(): pl.pallas_call(hand_over, out_shape=tuple((jax.ShapeDtypeStruct(r.shape,...  1.95 us

profile of v5, /device:TPU:1, one launch (start us, length us, event | category | flops | bytes accessed | tf_op | source)
XLA Modules:
  0.0 69.0 jit_solution(5625719032165486447)
XLA Ops:
  1.3 65.6 %shard_map.129 = (bf16[224,1024]{1,0:T(8,128)(2,1)}, f32[256,256]{1,0:T(8,128)}, f32[16,256]{1,0:T(8,128)}, f32[16,256]{1,0:T(8,128)}) custom-call(bf16[224,1024]{1,0:T(8,128)(2,1)} %bitcast.7, bf16[224,128]{1,0:T(8,128)(2,1)} %bitcast.9, bf16[224,128]{1,0:T(8,128)(2,1)} %bitcast.10, bf16[224,1024]{1,0:T(8,128)(2,1)} %bitcast.8, s32[1,224]{1,0:T(1,128)} %seg_row_ref.1, ...), custom_call_target="tpu_custom_call" | custom-call | tf_op jit(solution)/shard_map/pallas_call | solution.py:656
  66.9 1.9 %shard_map.130 = (bf16[224,1024]{1,0:T(8,128)(2,1)}, f32[256,256]{1,0:T(8,128)}, f32[16,256]{1,0:T(8,128)}, f32[16,256]{1,0:T(8,128)}) custom-call(bf16[224,1024]{1,0:T(8,128)(2,1)} %get-tuple-element.12.refs_0_, f32[256,256]{1,0:T(8,128)} %get-tuple-element.13.refs_1_, f32[16,256]{1,0:T(8,128)} %get-tuple-element.14.refs_2_, ...), custom_call_target="tpu_custom_call" | custom-call | tf_op jit(solution)/shard_map/pallas_call | solution.py:722
